TPU v7x, 32 devices: a whole 2x2x4 slice. The times are simulated.
32 devices in a mesh: ctx: 8 (over z, y), fsdp: 4 (over x, core).
Axes of the slice: x: 2, y: 2, z: 4, core: 2. Of those that a mesh axis runs over, the one named last changes fastest.
Arguments:
- inputs: bfloat16 [16, 1024, 640], P('fsdp', 'ctx'), may hold values from -6 to 6
- cotangent: bfloat16 [16, 1024, 640], P('fsdp', 'ctx'), may hold values from -6 to 6
- lengths: int32 [16], P('fsdp'), may hold values from 256 to 1024, as said below
- query_weight: bfloat16 [640, 1024], P('fsdp'), may hold values from -0.25 to 0.25
- key_weight: bfloat16 [640, 256], P('fsdp'), may hold values from -0.25 to 0.25
- value_weight: bfloat16 [640, 256], P('fsdp'), may hold values from -0.25 to 0.25
- out_weight: bfloat16 [1024, 640], P('fsdp'), may hold values from -0.1875 to 0.1875
- gate_weight: bfloat16 [640, 2048], P('fsdp'), may hold values from -0.25 to 0.25
- up_weight: bfloat16 [640, 2048], P('fsdp'), may hold values from -0.25 to 0.25
- down_weight: bfloat16 [2048, 640], P('fsdp'), may hold values from -0.125 to 0.125
- pre_attn_gain: bfloat16 [640], P('fsdp'), may hold values from -0.5 to 0.5
- post_attn_gain: bfloat16 [640], P('fsdp'), may hold values from -0.5 to 0.5
- pre_ffw_gain: bfloat16 [640], P('fsdp'), may hold values from -0.5 to 0.5
- post_ffw_gain: bfloat16 [640], P('fsdp'), may hold values from -0.5 to 0.5
- query_gain: bfloat16 [256], P('fsdp'), may hold values from 0 to 0.796875
- key_gain: bfloat16 [256], P('fsdp'), may hold values from 0 to 0.796875
Outputs:
- outputs: bfloat16 [16, 1024, 640], P('fsdp', 'ctx')
- input_grad: bfloat16 [16, 1024, 640], P('fsdp', 'ctx')
- query_weight_grad: float32 [640, 1024], P('fsdp')
- key_weight_grad: float32 [640, 256], P('fsdp')
- value_weight_grad: float32 [640, 256], P('fsdp')
- out_weight_grad: float32 [1024, 640], P('fsdp')
- gate_weight_grad: float32 [640, 2048], P('fsdp')
- up_weight_grad: float32 [640, 2048], P('fsdp')
- down_weight_grad: float32 [2048, 640], P('fsdp')
- pre_attn_gain_grad: float32 [640], P('fsdp')
- post_attn_gain_grad: float32 [640], P('fsdp')
- pre_ffw_gain_grad: float32 [640], P('fsdp')
- post_ffw_gain_grad: float32 [640], P('fsdp')
- query_gain_grad: float32 [256], P('fsdp')
- key_gain_grad: float32 [256], P('fsdp')
Inputs may be any that keep to these rules, and one draw needn't show every extreme that they name: Sequence s has its first lengths[s] positions live; later keys are excluded from every softmax. In each aligned block of 4 sequences exactly one, drawn from the seed, has all 1024 positions live.
All inputs are finite; a program needn't handle non-finite values.
Results may differ from a plain program's by a relative error of at most 0.022.
Values may be sent and summed in bfloat16 or wider, within the bound.
A program may use at most 256 MiB of HBM per device.

v0:
```python
import math
import jax
import jax.numpy as jnp
from jax import lax
from jax.sharding import PartitionSpec as P

EPSILON = 1e-06
MASKED_SCORE = -1e30
ROPE_BASE = 1000000.0


def norm_gain(values, gain_vec):
    return (
        values
        * lax.rsqrt(jnp.mean(values * values, axis=-1, keepdims=True) + EPSILON)
        * (1.0 + gain_vec)
    )


def rotate(values, positions):
    half_dim = values.shape[-1] // 2
    inverse = ROPE_BASE ** (-(jnp.arange(half_dim).astype(jnp.float32) * 2.0) / values.shape[-1])
    angles = positions.astype(jnp.float32)[:, None] * inverse[None, :]
    cosine = jnp.cos(angles)[:, None, :]
    sine_part = jnp.sin(angles)[:, None, :]
    first_half = values[..., :half_dim]
    second_half = values[..., half_dim:]
    return jnp.concatenate(
        [
            first_half * cosine - second_half * sine_part,
            second_half * cosine + first_half * sine_part,
        ],
        axis=-1,
    )


def gelu_mix(gate_in, up_in):
    return jax.nn.gelu(gate_in, approximate=True) * up_in


def body(
    inputs,
    cotangent,
    lengths,
    query_weight,
    key_weight,
    value_weight,
    out_weight,
    gate_weight,
    up_weight,
    down_weight,
    pre_attn_gain,
    post_attn_gain,
    pre_ffw_gain,
    post_ffw_gain,
    query_gain,
    key_gain,
):
    seq_count, row_count, model_width = inputs.shape
    gathered = (
        lax.all_gather(query_weight, "fsdp", axis=0, tiled=True),
        lax.all_gather(key_weight, "fsdp", axis=0, tiled=True),
        lax.all_gather(value_weight, "fsdp", axis=0, tiled=True),
        lax.all_gather(out_weight, "fsdp", axis=0, tiled=True),
        lax.all_gather(gate_weight, "fsdp", axis=0, tiled=True),
        lax.all_gather(up_weight, "fsdp", axis=0, tiled=True),
        lax.all_gather(down_weight, "fsdp", axis=0, tiled=True),
        lax.all_gather(pre_attn_gain, "fsdp", axis=0, tiled=True),
        lax.all_gather(post_attn_gain, "fsdp", axis=0, tiled=True),
        lax.all_gather(pre_ffw_gain, "fsdp", axis=0, tiled=True),
        lax.all_gather(post_ffw_gain, "fsdp", axis=0, tiled=True),
        lax.all_gather(query_gain, "fsdp", axis=0, tiled=True),
        lax.all_gather(key_gain, "fsdp", axis=0, tiled=True),
    )
    (
        query_full,
        key_full,
        value_full,
        out_full,
        gate_full,
        up_full,
        down_full,
        gain_attn_in,
        gain_attn_out,
        gain_ffw_in,
        gain_ffw_out,
        gain_query,
        gain_key,
    ) = gathered
    gain_attn_in = gain_attn_in.astype(jnp.float32)
    gain_attn_out = gain_attn_out.astype(jnp.float32)
    gain_ffw_in = gain_ffw_in.astype(jnp.float32)
    gain_ffw_out = gain_ffw_out.astype(jnp.float32)
    gain_query = gain_query.astype(jnp.float32)
    gain_key = gain_key.astype(jnp.float32)
    head_dim = key_full.shape[1]
    head_count = query_full.shape[1] // head_dim
    seq_len = row_count * lax.axis_size("ctx")
    key_span = math.gcd(512, seq_len)
    att_scale = head_dim ** (-0.5)
    flat_rows = seq_count * row_count
    positions = lax.axis_index("ctx") * row_count + jnp.arange(row_count, dtype=jnp.int32)
    x_flat = inputs.astype(jnp.float32).reshape(flat_rows, model_width)
    attn_in, attn_in_back = jax.vjp(norm_gain, x_flat, gain_attn_in)
    attn_in_b = attn_in.astype(jnp.bfloat16)
    query_lin = jnp.dot(attn_in_b, query_full, preferred_element_type=jnp.float32)
    key_lin = jnp.dot(attn_in_b, key_full, preferred_element_type=jnp.float32)
    value_lin = jnp.dot(attn_in_b, value_full, preferred_element_type=jnp.float32)

    def query_side(lin_values, gain_vec):
        return rotate(
            norm_gain(lin_values.reshape(seq_count, row_count, head_count, head_dim), gain_vec),
            positions,
        )

    def key_side(lin_values, gain_vec):
        return rotate(
            norm_gain(lin_values.reshape(seq_count, row_count, 1, head_dim), gain_vec), positions
        )[:, :, 0, :]

    query_rot, query_side_back = jax.vjp(query_side, query_lin, gain_query)
    key_rot, key_side_back = jax.vjp(key_side, key_lin, gain_key)
    query_b = query_rot.astype(jnp.bfloat16)
    key_b = key_rot.astype(jnp.bfloat16)
    value_b = value_lin.reshape(seq_count, row_count, head_dim).astype(jnp.bfloat16)

    def allowed(key_begin, key_count):
        key_pos = key_begin + jnp.arange(key_count, dtype=jnp.int32)
        causal = key_pos[None, :] <= positions[:, None]
        live = key_pos[None, :] < lengths[:, None]
        return (causal[None] & live[:, None, :])[:, None]

    def raw_scores(key_piece):
        return (
            jnp.einsum("sqhd,skd->shqk", query_b, key_piece, preferred_element_type=jnp.float32)
            * att_scale
        )

    stat_shape = (seq_count, head_count, row_count)
    running_max = jnp.full(stat_shape, MASKED_SCORE, jnp.float32)
    key_piece = lax.all_gather(key_b, "ctx", axis=1, tiled=True)
    value_piece = lax.all_gather(value_b, "ctx", axis=1, tiled=True)
    mask_now = allowed(jnp.int32(0), key_piece.shape[1])
    scores = jnp.where(mask_now, raw_scores(key_piece), MASKED_SCORE)
    new_max = jnp.maximum(running_max, jnp.max(scores, axis=-1))
    weights = jnp.where(mask_now, jnp.exp(scores - new_max[..., None]), 0.0)
    new_sum = jnp.sum(weights, axis=-1)
    new_acc = jnp.einsum(
        "shqk,skd->shqd",
        weights.astype(jnp.bfloat16),
        value_piece,
        preferred_element_type=jnp.float32,
    )
    final_state = (new_max, new_sum, new_acc)
    final_max, final_sum, final_acc = final_state
    attended = final_acc / final_sum[..., None]
    log_total = final_max + jnp.log(final_sum)
    attended_b = (
        attended.transpose(0, 2, 1, 3)
        .reshape(flat_rows, head_count * head_dim)
        .astype(jnp.bfloat16)
    )
    attn_lin = jnp.dot(attended_b, out_full, preferred_element_type=jnp.float32)
    attn_post, attn_post_back = jax.vjp(norm_gain, attn_lin, gain_attn_out)
    middle = x_flat + attn_post
    ffw_in, ffw_in_back = jax.vjp(norm_gain, middle, gain_ffw_in)
    ffw_in_b = ffw_in.astype(jnp.bfloat16)
    gate_lin = jnp.dot(ffw_in_b, gate_full, preferred_element_type=jnp.float32)
    up_lin = jnp.dot(ffw_in_b, up_full, preferred_element_type=jnp.float32)
    hidden, hidden_back = jax.vjp(gelu_mix, gate_lin, up_lin)
    hidden_b = hidden.astype(jnp.bfloat16)
    ffw_out = jnp.dot(hidden_b, down_full, preferred_element_type=jnp.float32)
    ffw_post, ffw_post_back = jax.vjp(norm_gain, ffw_out, gain_ffw_out)
    outputs = (middle + ffw_post).astype(jnp.bfloat16).reshape(seq_count, row_count, model_width)
    grad_top = cotangent.astype(jnp.float32).reshape(flat_rows, model_width)
    d_ffw_out, grad_ffw_out_gain = ffw_post_back(grad_top)
    d_ffw_out_b = d_ffw_out.astype(jnp.bfloat16)
    grad_down = jnp.einsum("rf,rd->fd", hidden_b, d_ffw_out_b, preferred_element_type=jnp.float32)
    d_hidden = jnp.einsum("rd,fd->rf", d_ffw_out_b, down_full, preferred_element_type=jnp.float32)
    d_gate, d_up = hidden_back(d_hidden)
    d_gate_b = d_gate.astype(jnp.bfloat16)
    d_up_b = d_up.astype(jnp.bfloat16)
    grad_gate = jnp.einsum("rd,rf->df", ffw_in_b, d_gate_b, preferred_element_type=jnp.float32)
    grad_up = jnp.einsum("rd,rf->df", ffw_in_b, d_up_b, preferred_element_type=jnp.float32)
    d_ffw_in = jnp.einsum(
        "rf,df->rd", d_gate_b, gate_full, preferred_element_type=jnp.float32
    ) + jnp.einsum("rf,df->rd", d_up_b, up_full, preferred_element_type=jnp.float32)
    d_middle_part, grad_ffw_in_gain = ffw_in_back(d_ffw_in)
    d_middle = grad_top + d_middle_part
    d_attn_lin, grad_attn_out_gain = attn_post_back(d_middle)
    d_attn_b = d_attn_lin.astype(jnp.bfloat16)
    grad_projection = jnp.einsum(
        "ro,rd->od", attended_b, d_attn_b, preferred_element_type=jnp.float32
    )
    d_attended_b = (
        jnp.einsum("rd,od->ro", d_attn_b, out_full, preferred_element_type=jnp.float32)
        .astype(jnp.bfloat16)
        .reshape(seq_count, row_count, head_count, head_dim)
    )
    d_attended = d_attended_b.astype(jnp.float32)
    row_delta = jnp.einsum("sqhd,shqd->shq", d_attended, attended, precision=lax.Precision.HIGHEST)

    def key_grads(key_piece, value_piece, key_begin):
        mask_now = allowed(key_begin, key_piece.shape[1])
        probabilities = jnp.where(
            mask_now, jnp.exp(raw_scores(key_piece) - log_total[..., None]), 0.0
        )
        d_probs = jnp.einsum(
            "sqhd,skd->shqk", d_attended_b, value_piece, preferred_element_type=jnp.float32
        )
        d_scores = (probabilities * (d_probs - row_delta[..., None])).astype(jnp.bfloat16)
        d_query = (
            jnp.einsum("shqk,skd->sqhd", d_scores, key_piece, preferred_element_type=jnp.float32)
            * att_scale
        )
        d_key = (
            jnp.einsum("shqk,sqhd->skd", d_scores, query_b, preferred_element_type=jnp.float32)
            * att_scale
        )
        d_value = jnp.einsum(
            "shqk,sqhd->skd",
            probabilities.astype(jnp.bfloat16),
            d_attended_b,
            preferred_element_type=jnp.float32,
        )
        return (d_query, jnp.concatenate([d_key, d_value], axis=-1))

    key_back_all, value_back_all = (
        lax.all_gather(key_b, "ctx", axis=1, tiled=True),
        lax.all_gather(value_b, "ctx", axis=1, tiled=True),
    )

    def slice_keys(key_begin, key_count):
        return (
            lax.dynamic_slice_in_dim(key_back_all, key_begin, key_count, 1),
            lax.dynamic_slice_in_dim(value_back_all, key_begin, key_count, 1),
        )

    query_zero = jnp.zeros((seq_count, row_count, head_count, head_dim), jnp.float32)

    def joint_step(block_id, state):
        d_query_sum, key_buffer = state
        key_begin = block_id * key_span
        key_piece, value_piece = slice_keys(key_begin, key_span)
        d_query, d_keyval = key_grads(key_piece, value_piece, key_begin)
        return (
            d_query_sum + d_query,
            lax.dynamic_update_slice_in_dim(key_buffer, d_keyval, key_begin, 1),
        )

    d_query_rot, key_buffer = lax.fori_loop(
        0,
        seq_len // key_span,
        joint_step,
        (query_zero, jnp.zeros((seq_count, seq_len, 2 * head_dim), jnp.float32)),
    )
    d_keyval_own = lax.psum_scatter(key_buffer, "ctx", scatter_dimension=1, tiled=True)
    d_key_rot = d_keyval_own[..., :head_dim]
    d_value = d_keyval_own[..., head_dim:]
    d_query_lin, grad_query_gain = query_side_back(d_query_rot)
    d_key_lin, grad_key_gain = key_side_back(d_key_rot)
    d_query_b = d_query_lin.astype(jnp.bfloat16)
    d_key_b = d_key_lin.astype(jnp.bfloat16)
    d_value_b = d_value.reshape(flat_rows, head_dim).astype(jnp.bfloat16)
    grad_query = jnp.einsum("rd,rq->dq", attn_in_b, d_query_b, preferred_element_type=jnp.float32)
    grad_key = jnp.einsum("rd,rq->dq", attn_in_b, d_key_b, preferred_element_type=jnp.float32)
    grad_value = jnp.einsum("rd,rq->dq", attn_in_b, d_value_b, preferred_element_type=jnp.float32)
    d_attn_in = jnp.einsum("rq,dq->rd", d_query_b, query_full, preferred_element_type=jnp.float32)
    d_attn_in = d_attn_in + jnp.einsum(
        "rq,dq->rd", d_key_b, key_full, preferred_element_type=jnp.float32
    )
    d_attn_in = d_attn_in + jnp.einsum(
        "rq,dq->rd", d_value_b, value_full, preferred_element_type=jnp.float32
    )
    d_input_part, grad_attn_in_gain = attn_in_back(d_attn_in)
    input_grad = (
        (d_middle + d_input_part).astype(jnp.bfloat16).reshape(seq_count, row_count, model_width)
    )
    shards = (
        lax.psum_scatter(
            grad_query.astype(jnp.bfloat16), "fsdp", scatter_dimension=0, tiled=True
        ).astype(jnp.float32),
        lax.psum_scatter(
            grad_key.astype(jnp.bfloat16), "fsdp", scatter_dimension=0, tiled=True
        ).astype(jnp.float32),
        lax.psum_scatter(
            grad_value.astype(jnp.bfloat16), "fsdp", scatter_dimension=0, tiled=True
        ).astype(jnp.float32),
        lax.psum_scatter(
            grad_projection.astype(jnp.bfloat16), "fsdp", scatter_dimension=0, tiled=True
        ).astype(jnp.float32),
        lax.psum_scatter(
            grad_gate.astype(jnp.bfloat16), "fsdp", scatter_dimension=0, tiled=True
        ).astype(jnp.float32),
        lax.psum_scatter(
            grad_up.astype(jnp.bfloat16), "fsdp", scatter_dimension=0, tiled=True
        ).astype(jnp.float32),
        lax.psum_scatter(
            grad_down.astype(jnp.bfloat16), "fsdp", scatter_dimension=0, tiled=True
        ).astype(jnp.float32),
        lax.psum_scatter(
            grad_attn_in_gain.astype(jnp.bfloat16), "fsdp", scatter_dimension=0, tiled=True
        ).astype(jnp.float32),
        lax.psum_scatter(
            grad_attn_out_gain.astype(jnp.bfloat16), "fsdp", scatter_dimension=0, tiled=True
        ).astype(jnp.float32),
        lax.psum_scatter(
            grad_ffw_in_gain.astype(jnp.bfloat16), "fsdp", scatter_dimension=0, tiled=True
        ).astype(jnp.float32),
        lax.psum_scatter(
            grad_ffw_out_gain.astype(jnp.bfloat16), "fsdp", scatter_dimension=0, tiled=True
        ).astype(jnp.float32),
        lax.psum_scatter(
            grad_query_gain.astype(jnp.bfloat16), "fsdp", scatter_dimension=0, tiled=True
        ).astype(jnp.float32),
        lax.psum_scatter(
            grad_key_gain.astype(jnp.bfloat16), "fsdp", scatter_dimension=0, tiled=True
        ).astype(jnp.float32),
    )
    totals = lax.psum(
        (
            shards[0],
            shards[1],
            shards[2],
            shards[3],
            shards[4],
            shards[5],
            shards[6],
            shards[7],
            shards[8],
            shards[9],
            shards[10],
            shards[11],
            shards[12],
        ),
        "ctx",
    )
    return (outputs, input_grad) + tuple(totals)


def solution(mesh):
    in_specs = (
        P("fsdp", "ctx", None),
        P("fsdp", "ctx", None),
        P("fsdp"),
        P("fsdp", None),
        P("fsdp", None),
        P("fsdp", None),
        P("fsdp", None),
        P("fsdp", None),
        P("fsdp", None),
        P("fsdp", None),
        P("fsdp"),
        P("fsdp"),
        P("fsdp"),
        P("fsdp"),
        P("fsdp"),
        P("fsdp"),
    )
    out_specs = (
        P("fsdp", "ctx", None),
        P("fsdp", "ctx", None),
        P("fsdp", None),
        P("fsdp", None),
        P("fsdp", None),
        P("fsdp", None),
        P("fsdp", None),
        P("fsdp", None),
        P("fsdp", None),
        P("fsdp"),
        P("fsdp"),
        P("fsdp"),
        P("fsdp"),
        P("fsdp"),
        P("fsdp"),
    )
    return jax.shard_map(body, mesh=mesh, in_specs=in_specs, out_specs=out_specs, check_vma=False)
```

profile of v0, /device:TPU:0, one launch (start us, length us, event | category | flops | bytes accessed | tf_op | source)
XLA Modules:
  0.0 893.9 jit_solution(16385621297810421104)
XLA Ops:
  17.0 9.2 %all-reduce.18 = (bf16[256]{0:T(256)(128)(2,1)S(1)}, bf16[640]{0:T(1024)(128)(2,1)S(1)}, bf16[256]{0:T(256)(128)(2,1)S(1)}, bf16[640]{0:T(1024)(128)(2,1)S(1)}, ...) all-reduce(bf16[256]{0:T(256)(128)(2,1)S(1)} %dynamic-update-slice., ...), channel_id=1, replica_groups=mesh['ctx'=8,'fsdp'=4] {'fsdp'}, use_global_device_ids=true, to_apply=%add.5 | all-reduce | flops 3072 | bytes 12288
  26.3 6.2 all_gather.48
  36.3 6.2 all_gather.53
  48.5 2.4 copy.67
  50.9 2.4 multiply_reduce_fusion.3
  58.8 27.3 %all-gather.21.cloned.1.call-done = bf16[4,1024,1,256]{3,1,0,2:T(8,128)(2,1)} async-done(((bf16[4,128,1,256]{3,1,0,2:T(8,128)(2,1)}), bf16[4,1024,1,256]{3,1,0,2:T(8,128)(2,1)}) %all-gather.21.cloned.1.call-update) | async-done | bytes 2097168 | tf_op jit(solution)/shard_map/all_gather | solution.py:141
  86.0 3.3 fusion.28
  89.4 3.2 copy-done.16
  92.7 2.2 fusion.29
  94.9 41.7 %all-gather.11.cloned.1.call-done = bf16[4,1024,256]{2,1,0:T(8,128)(2,1)} async-done(((bf16[4,128,256]{2,1,0:T(8,128)(2,1)}), bf16[4,1024,256]{2,1,0:T(8,128)(2,1)}) %all-gather.11.cloned.1.call-update) | async-done | bytes 2097168 | tf_op jit(solution)/shard_map/all_gather | solution.py:142
  136.6 8.1 fusion.45
  146.8 8.0 all-gather.13.cloned.1.call-done
  154.7 2.8 multiply_reduce_fusion.10
  160.6 21.1 %all-gather.15.cloned.1.call-done = bf16[640,2048]{1,0:T(8,128)(2,1)} async-done(((bf16[160,2048]{1,0:T(8,128)(2,1)}), bf16[640,2048]{1,0:T(8,128)(2,1)}) %all-gather.15.cloned.1.call-update) | async-done | bytes 2621456 | tf_op jit(solution)/shard_map/all_gather | solution.py:65
  181.7 5.8 fusion.78
  187.5 21.2 %all-gather.17.cloned.1.call-done = bf16[640,2048]{1,0:T(8,128)(2,1)} async-done(((bf16[160,2048]{1,0:T(8,128)(2,1)}), bf16[640,2048]{1,0:T(8,128)(2,1)}) %all-gather.17.cloned.1.call-update) | async-done | bytes 2621456 | tf_op jit(solution)/shard_map/all_gather | solution.py:66
  208.7 8.3 multiply_convert_fusion.1
  217.0 18.9 %all-gather.19.cloned.1.call-done = bf16[2048,640]{1,0:T(8,128)(2,1)} async-done(((bf16[512,640]{1,0:T(8,128)(2,1)}), bf16[2048,640]{1,0:T(8,128)(2,1)}) %all-gather.19.cloned.1.call-update) | async-done | bytes 2621456 | tf_op jit(solution)/shard_map/all_gather | solution.py:67
  235.9 4.4 multiply_reduce_fusion.8
  243.6 4.8 multiply_convert_fusion
  251.7 2.1 multiply_reduce_fusion.4
  258.7 3.5 convolution_convert_fusion.5
  262.2 2.6 reshape.457
  264.8 2.4 copy.71
  267.2 2.9 bitcast_convert_fusion
  270.3 3.0 multiply_reduce_fusion
  273.3 4.3 broadcast_in_dim.140.clone
  277.6 40.3 %while.16 = (s32[]{:T(128)}, f32[4,128,4,256]{1,3,2,0:T(8,128)S(1)}, f32[4,1024,512]{2,1,0:T(8,128)}, bf16[4,1024,256]{2,1,0:T(8,128)(2,1)}, s32[4]{0:T(128)S(1)...) while((s32[]{:T(128)}, ...), condition=%wide.region_12.13_spmd.clone, body=%wide.region_11.12_spmd.clone.sunk | while | flops 2698316288 | bytes 81694016 | solution.py:251
  285.7 2.4 pad_maximum_fusion.5
  288.1 5.3 copy.128
  293.4 4.6 constant_dynamic-update-slice_fusion.2
  305.6 2.4 pad_maximum_fusion.5
  308.0 5.3 copy.128
  313.3 4.6 constant_dynamic-update-slice_fusion.2
  327.6 4.6 convolution_convert_fusion.2
  332.5 4.8 convolution_convert_fusion.1
  338.3 4.9 convolution_convert_fusion
  345.4 3.3 fusion.80
  348.7 5.6 reduce-scatter.11.cloned.1.call-done
  354.4 37.1 %reduce-scatter.19.cloned.1.call-done = bf16[160,2048]{1,0:T(8,128)(2,1)} async-done(((bf16[640,2048]{1,0:T(8,128)(2,1)}), bf16[160,2048]{1,0:T(8,128)(2,1)}) %reduce-scatter.19.cloned.1.call-update) | async-done | bytes 655376 | tf_op jit(solution)/shard_map/reduce_scatter | solution.py:292
  391.5 37.4 %reduce-scatter.21.cloned.1.call-done = bf16[160,2048]{1,0:T(8,128)(2,1)} async-done(((bf16[640,2048]{1,0:T(8,128)(2,1)}), bf16[160,2048]{1,0:T(8,128)(2,1)}) %reduce-scatter.21.cloned.1.call-update) | async-done | bytes 655376 | tf_op jit(solution)/shard_map/reduce_scatter | solution.py:295
  428.9 37.1 %reduce-scatter.23.cloned.1.call-done = bf16[512,640]{1,0:T(8,128)(2,1)} async-done(((bf16[2048,640]{1,0:T(8,128)(2,1)}), bf16[512,640]{1,0:T(8,128)(2,1)}) %reduce-scatter.23.cloned.1.call-update) | async-done | bytes 655376 | tf_op jit(solution)/shard_map/reduce_scatter | solution.py:298
  466.0 153.5 %reduce-scatter.9.cloned.1.call-done = f32[4,128,512]{2,1,0:T(8,128)} async-done(((f32[4,1024,512]{2,1,0:T(8,128)}), f32[4,128,512]{2,1,0:T(8,128)}) %reduce-scatter.9.cloned.1.call-update) | async-done | bytes 1048592 | tf_op jit(solution)/shard_map/reduce_scatter | solution.py:257
  627.2 7.1 all-reduce.17
  635.9 2.7 fusion.52
  638.6 3.3 reduce-scatter.15.cloned.1.call-done
  641.9 23.6 %reduce-scatter.13.cloned.1.call-done = bf16[160,256]{1,0:T(8,128)(2,1)} async-done(((bf16[640,256]{1,0:T(8,128)(2,1)}), bf16[160,256]{1,0:T(8,128)(2,1)}) %reduce-scatter.13.cloned.1.call-update) | async-done | bytes 81936 | tf_op jit(solution)/shard_map/reduce_scatter | solution.py:283
  665.5 221.7 %all-reduce.20 = (f32[160,1024]{1,0:T(8,128)}, f32[160,256]{1,0:T(8,128)}, f32[160,256]{1,0:T(8,128)}, f32[256,640]{1,0:T(8,128)}, f32[160,2048]{1,0:T(8,128)}, ...) all-reduce(bf16[160,1024]{1,0:T(8,128)(2,1)} %reduce-scatter.11.clo, ...), channel_id=1, replica_groups=mesh['ctx'=8,'fsdp'=4] {'ctx'}, use_global_device_ids=true, to_apply=%region_18.19 | all-reduce | flops 1393408 | bytes 8361984 | tf_op jit(solution)/shard_map/psum | solution.py:320
  (278 shorter events, 75.7 us)
Async XLA Ops:
  7.2 41.3 %all-gather.9.cloned.1.call-start = ((), (), s32[]{:S(2)}) async-start(), calls=%async_computation.8 | async-start | bytes 1638400 | tf_op jit(solution)/shard_map/all_gather | solution.py:61
  7.9 78.1 %all-gather.21.cloned.1.call-start = ((), (), s32[]{:S(2)}) async-start(), calls=%async_computation.22 | async-start | bytes 2359296 | tf_op jit(solution)/shard_map/all_gather | solution.py:141
  11.9 30.6 %copy-start.51 = (f32[4,128]{1,0:T(4,128)}, f32[4,128]{1,0:T(4,128)S(1)}, u32[]{:S(2)}) copy-start(f32[4,128]{1,0:T(4,128)S(1)} %fusion.58) | copy-start | bytes 6148
  11.9 20.5 %copy-start.47 = (f32[512]{0:T(512)}, f32[512]{0:T(512)S(1)}, u32[]{:S(2)}) copy-start(f32[512]{0:T(512)S(1)} %bitcast_rsqrt_fusion.1) | copy-start | bytes 6148
  26.2 9.1 %copy-start.56 = (f32[256]{0:T(256)}, f32[256]{0:T(256)S(1)}, u32[]{:S(2)}) copy-start(f32[256]{0:T(256)S(1)} %convert_add_fusion.6) | copy-start | bytes 3076
  32.4 3.0 copy-start.20
  32.4 10.0 %copy-start.42 = (f32[640]{0:T(1024)}, f32[640]{0:T(1024)S(1)}, u32[]{:S(2)}) copy-start(f32[640]{0:T(1024)S(1)} %convert_add_fusion.4) | copy-start | bytes 7684
  33.9 2.4 copy-start.44
  33.9 8.6 copy-start.3
  34.7 19.6 %copy-start.25 = (f32[128,128]{1,0:T(8,128)}, f32[128,128]{1,0:T(8,128)S(1)}, u32[]{:S(2)}) copy-start(f32[128,128]{1,0:T(8,128)S(1)} %get-tuple-element.348) | copy-start | bytes 196612
  34.7 19.6 %copy-start.27 = (f32[128,128]{1,0:T(8,128)}, f32[128,128]{1,0:T(8,128)S(1)}, u32[]{:S(2)}) copy-start(f32[128,128]{1,0:T(8,128)S(1)} %get-tuple-element.349) | copy-start | bytes 196612
  36.2 100.4 %all-gather.11.cloned.1.call-start = ((), (), s32[]{:S(2)}) async-start(), calls=%async_computation.9 | async-start | bytes 2359296 | tf_op jit(solution)/shard_map/all_gather | solution.py:142
  42.5 3.1 copy-start.18
  42.7 8.2 copy-start.14
  42.7 3.7 copy-start.55
  43.9 110.9 %all-gather.13.cloned.1.call-start = ((), (), s32[]{:S(2)}) async-start(), calls=%async_computation.10 | async-start | bytes 1638400 | tf_op jit(solution)/shard_map/all_gather | solution.py:64
  44.4 137.3 %all-gather.15.cloned.1.call-start = ((), (), s32[]{:S(2)}) async-start(), calls=%async_computation.11 | async-start | bytes 3276800 | tf_op jit(solution)/shard_map/all_gather | solution.py:65
  45.0 163.7 %all-gather.17.cloned.1.call-start = ((), (), s32[]{:S(2)}) async-start(), calls=%async_computation.12 | async-start | bytes 3276800 | tf_op jit(solution)/shard_map/all_gather | solution.py:66
  45.6 190.3 %all-gather.19.cloned.1.call-start = ((), (), s32[]{:S(2)}) async-start(), calls=%async_computation.13 | async-start | bytes 3276800 | tf_op jit(solution)/shard_map/all_gather | solution.py:67
  46.4 302.3 %reduce-scatter.17.cloned.1.call-start = ((), (), s32[]{:S(2)}) async-start(), calls=%async_computation.18 | async-start | bytes 1638400 | tf_op jit(solution)/shard_map/reduce_scatter | solution.py:289
  46.4 7.5 copy-start.58
  86.0 6.6 copy-start.22
  89.4 3.3 copy-start.16
  154.7 2.8 copy-start.4
  235.9 4.4 copy-start.17
  235.9 7.1 copy-start.64
  235.9 7.1 copy-start.67
  243.0 5.4 copy-start.34
  243.6 4.9 copy-start.60
  248.5 3.2 copy-start.61
  270.2 84.1 %reduce-scatter.11.cloned.1.call-start = ((), (), s32[]{:S(2)}) async-start(), calls=%async_computation.15 | async-start | bytes 1638400 | tf_op jit(solution)/shard_map/reduce_scatter | solution.py:280
  327.6 63.9 %reduce-scatter.19.cloned.1.call-start = ((), (), s32[]{:S(2)}) async-start(), calls=%async_computation.19 | async-start | bytes 3276800 | tf_op jit(solution)/shard_map/reduce_scatter | solution.py:292
  332.3 96.6 %reduce-scatter.21.cloned.1.call-start = ((), (), s32[]{:S(2)}) async-start(), calls=%async_computation.20 | async-start | bytes 3276800 | tf_op jit(solution)/shard_map/reduce_scatter | solution.py:295
  337.3 128.8 %reduce-scatter.23.cloned.1.call-start = ((), (), s32[]{:S(2)}) async-start(), calls=%async_computation.21 | async-start | bytes 3276800 | tf_op jit(solution)/shard_map/reduce_scatter | solution.py:298
  343.3 276.2 %reduce-scatter.9.cloned.1.call-start = ((), (), s32[]{:S(2)}) async-start(), calls=%async_computation.14 | async-start | bytes 9437184 | tf_op jit(solution)/shard_map/reduce_scatter | solution.py:257
  344.0 297.9 %reduce-scatter.15.cloned.1.call-start = ((), (), s32[]{:S(2)}) async-start(), calls=%async_computation.17 | async-start | bytes 409600 | tf_op jit(solution)/shard_map/reduce_scatter | solution.py:286
  348.7 273.4 %copy-start.9 = (f32[512,256]{1,0:T(8,128)S(1)}, f32[512,256]{1,0:T(8,128)}, u32[]{:S(2)}) copy-start(f32[512,256]{1,0:T(8,128)} %copy-done.8) | copy-start | bytes 1572868
  348.7 273.4 %copy-start.50 = (f32[4,128]{1,0:T(4,128)S(1)}, f32[4,128]{1,0:T(4,128)}, u32[]{:S(2)}) copy-start(f32[4,128]{1,0:T(4,128)} %copy-done.49) | copy-start | bytes 6148
  348.7 273.4 %copy-start.57 = (f32[256]{0:T(256)S(1)}, f32[256]{0:T(256)}, u32[]{:S(2)}) copy-start(f32[256]{0:T(256)} %copy-done.56) | copy-start | bytes 3076
  622.0 43.4 %reduce-scatter.13.cloned.1.call-start = ((), (), s32[]{:S(2)}) async-start(), calls=%async_computation.16 | async-start | bytes 409600 | tf_op jit(solution)/shard_map/reduce_scatter | solution.py:283
  622.6 2.9 copy-start.5
  622.6 2.9 copy-start.19
  622.6 2.9 copy-start.43
  622.6 2.9 copy-start.48
  625.6 10.4 %copy-start.52 = (f32[4,128]{1,0:T(4,128)S(1)}, f32[4,128]{1,0:T(4,128)}, u32[]{:S(2)}) copy-start(f32[4,128]{1,0:T(4,128)} %copy-done.51) | copy-start | bytes 6148
  625.6 10.4 %copy-start.13 = (f32[512,640]{1,0:T(8,128)S(1)}, f32[512,640]{1,0:T(8,128)}, u32[]{:S(2)}) copy-start(f32[512,640]{1,0:T(8,128)} %copy-done.12) | copy-start | bytes 3932164
  635.7 29.7 %copy-start.36 = (bf16[160,2048]{1,0:T(8,128)(2,1)S(1)}, bf16[160,2048]{1,0:T(8,128)(2,1)}, u32[]{:S(2)}) copy-start(bf16[160,2048]{1,0:T(8,128)(2,1)} %reduce-scatter.19.cloned.1.call-done) | copy-start | bytes 1966084
  635.7 29.7 %copy-start.37 = (bf16[160,2048]{1,0:T(8,128)(2,1)S(1)}, bf16[160,2048]{1,0:T(8,128)(2,1)}, u32[]{:S(2)}) copy-start(bf16[160,2048]{1,0:T(8,128)(2,1)} %reduce-scatter.21.cloned.1.call-done) | copy-start | bytes 1966084
  (38 other events, 60.4 us)
Sparse Core Ops, SparseCore 0:
  9.6 21.7 all-gather.8
  36.3 49.7 all-gather.20
  88.8 47.7 all-gather.10
  138.0 16.6 all-gather.12
  156.1 25.5 all-gather.14
  183.1 25.5 all-gather.16
  210.3 25.5 all-gather.18
  270.3 26.5 reduce-scatter.16
  327.7 26.6 reduce-scatter.10
  356.7 34.6 reduce-scatter.18
  394.2 34.6 reduce-scatter.20
  431.3 34.6 reduce-scatter.22
  470.1 149.3 reduce-scatter.8
  622.4 19.4 reduce-scatter.14
  645.0 20.4 reduce-scatter.12
where the time goes:
time: 902 us; the launch traced here: 894 us
  waiting for transfers between devices  440 us (49%)
  blocking collectives  250 us (28%)
  matrix products  88.8 us (10%)
  local copies, waits for them, and re-layouts  62.2 us (7%)
  other arithmetic  33.9 us (4%)
  between operations  17.6 us (2%)
    psum x1, blocking collectives, body(): lax.psum((shards[0], shards[1], shards[2], shards[3], shards[4], shards[5...  222 us
    reduce_scatter x1, waiting for transfers between devices, body(): lax.psum_scatter(key_buffer, 'ctx', scatter_dimension=1, tiled=True)  153 us
    all_gather x1, waiting for transfers between devices, body(): value_piece = lax.all_gather(value_b, 'ctx', axis=1, tiled=True)  41.7 us
    reduce_scatter x1, waiting for transfers between devices, body(): lax.psum_scatter(grad_up.astype(jnp.bfloat16), 'fsdp', scatter_dimension=...  37.4 us
    reduce_scatter x1, waiting for transfers between devices, body(): lax.psum_scatter(grad_down.astype(jnp.bfloat16), 'fsdp', scatter_dimensio...  37.1 us
    reduce_scatter x1, waiting for transfers between devices, body(): lax.psum_scatter(grad_gate.astype(jnp.bfloat16), 'fsdp', scatter_dimensio...  37.1 us
    all_gather x1, waiting for transfers between devices, body(): key_piece = lax.all_gather(key_b, 'ctx', axis=1, tiled=True)  27.3 us
    unnamed x147, local copies, waits for them, and re-layouts  25.9 us
  transfers between devices with their start and end apart: 15, of which 13 were waited for; matrix products, arithmetic and copies ran while one was open for 15% of the time, Pallas kernels for 0%

commit v1 on v0

--- a/solution.py
+++ b/solution.py
@@ -138,8 +138,11 @@
 
     stat_shape = (seq_count, head_count, row_count)
     running_max = jnp.full(stat_shape, MASKED_SCORE, jnp.float32)
-    key_piece = lax.all_gather(key_b, "ctx", axis=1, tiled=True)
-    value_piece = lax.all_gather(value_b, "ctx", axis=1, tiled=True)
+    key_piece, value_piece = jnp.split(
+        lax.all_gather(jnp.concatenate([key_b, value_b], 0), "ctx", tiled=True, axis=1),
+        [key_b.shape[0]],
+        axis=0,
+    )
     mask_now = allowed(jnp.int32(0), key_piece.shape[1])
     scores = jnp.where(mask_now, raw_scores(key_piece), MASKED_SCORE)
     new_max = jnp.maximum(running_max, jnp.max(scores, axis=-1))

time: 902 us -> 947 us (1.050)
  waiting for transfers between devices: 440 us -> 490 us
    all_gather x2 -> x3, waiting for transfers between devices: 69 us -> 122 us  [the longest x1 57.5 us: body(): lax.all_gather(jnp.concatenate([key_b, value_b], 0), 'ctx', tiled=True, a...]
    unnamed x147 -> x149, local copies, waits for them, and re-layouts: 25.9 us -> 22.4 us
  transfers between devices with their start and end apart: 15 -> 16, of which waited for: 13 -> 14; matrix products, arithmetic and copies ran while one was open for 15% -> 17% of each run, Pallas kernels for 0% -> 0%
where the time goes in v1:
time: 947 us; the launch traced here: 937 us
  waiting for transfers between devices  490 us (52%)
  blocking collectives  250 us (26%)
  matrix products  84.7 us (9%)
  local copies, waits for them, and re-layouts  58.8 us (6%)
  other arithmetic  34.5 us (4%)
  between operations  17.7 us (2%)
    psum x1, blocking collectives, body(): lax.psum((shards[0], shards[1], shards[2], shards[3], shards[4], shards[5...  222 us
    reduce_scatter x1, waiting for transfers between devices, body(): lax.psum_scatter(key_buffer, 'ctx', scatter_dimension=1, tiled=True)  153 us
    all_gather x1, waiting for transfers between devices, body(): lax.all_gather(jnp.concatenate([key_b, value_b], 0), 'ctx', tiled=True, a...  57.5 us
    all_gather x1, waiting for transfers between devices, body(): lax.all_gather(key_b, 'ctx', axis=1, tiled=True)  50 us
    reduce_scatter x1, waiting for transfers between devices, body(): lax.psum_scatter(grad_gate.astype(jnp.bfloat16), 'fsdp', scatter_dimensio...  37.3 us
    reduce_scatter x1, waiting for transfers between devices, body(): lax.psum_scatter(grad_up.astype(jnp.bfloat16), 'fsdp', scatter_dimension=...  37.3 us
    reduce_scatter x1, waiting for transfers between devices, body(): lax.psum_scatter(grad_down.astype(jnp.bfloat16), 'fsdp', scatter_dimensio...  37.2 us
    reduce_scatter x1, waiting for transfers between devices, body(): lax.psum_scatter(grad_key.astype(jnp.bfloat16), 'fsdp', scatter_dimension...  23.6 us
  transfers between devices with their start and end apart: 16, of which 14 were waited for; matrix products, arithmetic and copies ran while one was open for 17% of the time, Pallas kernels for 0%

profile of v1, /device:TPU:0, one launch (start us, length us, event | category | flops | bytes accessed | tf_op | source)
XLA Modules:
  0.0 937.4 jit_solution(4269235646652778134)
XLA Ops:
  17.0 9.2 all-reduce.18
  26.2 6.2 all_gather.49
  35.8 6.2 all_gather.51
  49.7 2.4 copy.67
  52.2 2.4 multiply_reduce_fusion.3
  60.1 57.5 %all-gather.10.cloned.1.call-done = bf16[8,1024,256]{2,1,0:T(8,128)(2,1)} async-done(((bf16[8,128,256]{2,1,0:T(8,128)(2,1)}), bf16[8,1024,256]{2,1,0:T(8,128)(2,1)}) %all-gather.10.cloned.1.call-update) | async-done | bytes 4194320 | tf_op jit(solution)/shard_map/all_gather | solution.py:142
  117.6 3.3 fusion.28
  123.1 4.3 fusion.43
  129.5 6.2 all-gather.14.cloned.1.call-done
  135.6 2.8 multiply_reduce_fusion.10
  141.5 21.1 %all-gather.16.cloned.1.call-done = bf16[640,2048]{1,0:T(8,128)(2,1)} async-done(((bf16[160,2048]{1,0:T(8,128)(2,1)}), bf16[640,2048]{1,0:T(8,128)(2,1)}) %all-gather.16.cloned.1.call-update) | async-done | bytes 2621456 | tf_op jit(solution)/shard_map/all_gather | solution.py:65
  162.6 5.8 fusion.77
  168.4 21.2 %all-gather.18.cloned.1.call-done = bf16[640,2048]{1,0:T(8,128)(2,1)} async-done(((bf16[160,2048]{1,0:T(8,128)(2,1)}), bf16[640,2048]{1,0:T(8,128)(2,1)}) %all-gather.18.cloned.1.call-update) | async-done | bytes 2621456 | tf_op jit(solution)/shard_map/all_gather | solution.py:66
  189.6 8.3 multiply_convert_fusion.1
  197.9 18.7 %all-gather.20.cloned.1.call-done = bf16[2048,640]{1,0:T(8,128)(2,1)} async-done(((bf16[512,640]{1,0:T(8,128)(2,1)}), bf16[2048,640]{1,0:T(8,128)(2,1)}) %all-gather.20.cloned.1.call-update) | async-done | bytes 2621456 | tf_op jit(solution)/shard_map/all_gather | solution.py:67
  216.7 4.4 multiply_reduce_fusion.8
  224.3 4.8 multiply_convert_fusion
  232.5 2.1 multiply_reduce_fusion.4
  239.4 2.6 reshape.457
  242.0 2.4 copy.71
  244.4 3.7 convolution_convert_fusion.3
  248.1 2.8 bitcast_convert_fusion
  251.0 3.0 multiply_reduce_fusion
  254.1 14.1 %all-gather.22.cloned.1.call-done = bf16[4,1024,256]{2,1,0:T(8,128)(2,1)} async-done(((bf16[4,128,256]{2,1,0:T(8,128)(2,1)}), bf16[4,1024,256]{2,1,0:T(8,128)(2,1)}) %all-gather.22.cloned.1.call-update) | async-done | bytes 2097168 | tf_op jit(solution)/shard_map/all_gather | solution.py:233
  268.1 50.0 %all-gather.24.cloned.1.call-done = bf16[4,1024,1,256]{3,1,0,2:T(8,128)(2,1)} async-done(((bf16[4,128,1,256]{3,1,0,2:T(8,128)(2,1)}), bf16[4,1024,1,256]{3,1,0,2:T(8,128)(2,1)}) %all-gather.24.cloned.1.call-update) | async-done | bytes 2097168 | tf_op jit(solution)/shard_map/all_gather | solution.py:232
  318.1 4.3 broadcast_in_dim.140.clone
  322.5 40.5 %while.16 = (s32[]{:T(128)}, f32[4,128,4,256]{1,3,2,0:T(8,128)S(1)}, f32[4,1024,512]{2,1,0:T(8,128)}, bf16[4,1024,256]{2,1,0:T(8,128)(2,1)}, s32[4]{0:T(128)S(1)...) while((s32[]{:T(128)}, ...), condition=%wide.region_12.13_spmd.clone, body=%wide.region_11.12_spmd.clone.sunk | while | flops 2698316288 | bytes 81694016 | solution.py:254
  323.5 2.3 fusion.148
  330.7 2.4 pad_maximum_fusion.6
  333.1 5.3 copy.128
  338.4 4.7 constant_dynamic-update-slice_fusion.2
  350.7 2.4 pad_maximum_fusion.6
  353.1 5.3 copy.128
  358.4 4.6 constant_dynamic-update-slice_fusion.2
  372.6 4.6 convolution_convert_fusion.2
  377.5 4.9 convolution_convert_fusion.1
  383.5 4.9 convolution_convert_fusion
  390.4 3.3 fusion.79
  393.7 4.1 reduce-scatter.11.cloned.1.call-done
  397.8 37.3 %reduce-scatter.19.cloned.1.call-done = bf16[160,2048]{1,0:T(8,128)(2,1)} async-done(((bf16[640,2048]{1,0:T(8,128)(2,1)}), bf16[160,2048]{1,0:T(8,128)(2,1)}) %reduce-scatter.19.cloned.1.call-update) | async-done | bytes 655376 | tf_op jit(solution)/shard_map/reduce_scatter | solution.py:295
  435.1 37.3 %reduce-scatter.21.cloned.1.call-done = bf16[160,2048]{1,0:T(8,128)(2,1)} async-done(((bf16[640,2048]{1,0:T(8,128)(2,1)}), bf16[160,2048]{1,0:T(8,128)(2,1)}) %reduce-scatter.21.cloned.1.call-update) | async-done | bytes 655376 | tf_op jit(solution)/shard_map/reduce_scatter | solution.py:298
  472.4 37.2 %reduce-scatter.23.cloned.1.call-done = bf16[512,640]{1,0:T(8,128)(2,1)} async-done(((bf16[2048,640]{1,0:T(8,128)(2,1)}), bf16[512,640]{1,0:T(8,128)(2,1)}) %reduce-scatter.23.cloned.1.call-update) | async-done | bytes 655376 | tf_op jit(solution)/shard_map/reduce_scatter | solution.py:301
  509.6 153.3 %reduce-scatter.9.cloned.1.call-done = f32[4,128,512]{2,1,0:T(8,128)} async-done(((f32[4,1024,512]{2,1,0:T(8,128)}), f32[4,128,512]{2,1,0:T(8,128)}) %reduce-scatter.9.cloned.1.call-update) | async-done | bytes 1048592 | tf_op jit(solution)/shard_map/reduce_scatter | solution.py:260
  670.7 7.1 all-reduce.17
  679.4 2.7 fusion.50
  682.1 3.2 reduce-scatter.15.cloned.1.call-done
  685.3 23.6 %reduce-scatter.13.cloned.1.call-done = bf16[160,256]{1,0:T(8,128)(2,1)} async-done(((bf16[640,256]{1,0:T(8,128)(2,1)}), bf16[160,256]{1,0:T(8,128)(2,1)}) %reduce-scatter.13.cloned.1.call-update) | async-done | bytes 81936 | tf_op jit(solution)/shard_map/reduce_scatter | solution.py:286
  708.9 221.7 %all-reduce.20 = (f32[160,1024]{1,0:T(8,128)}, f32[160,256]{1,0:T(8,128)}, f32[160,256]{1,0:T(8,128)}, f32[256,640]{1,0:T(8,128)}, f32[160,2048]{1,0:T(8,128)}, ...) all-reduce(bf16[160,1024]{1,0:T(8,128)(2,1)} %reduce-scatter.11.clo, ...), channel_id=1, replica_groups=mesh['ctx'=8,'fsdp'=4] {'ctx'}, use_global_device_ids=true, to_apply=%region_18.19 | all-reduce | flops 1393408 | bytes 8361984 | tf_op jit(solution)/shard_map/psum | solution.py:323
  (284 shorter events, 76.7 us)
Async XLA Ops:
  7.2 42.6 %all-gather.12.cloned.1.call-start = ((), (), s32[]{:S(2)}) async-start(), calls=%async_computation.9 | async-start | bytes 1638400 | tf_op jit(solution)/shard_map/all_gather | solution.py:61
  7.9 109.7 %all-gather.10.cloned.1.call-start = ((), (), s32[]{:S(2)}) async-start(), calls=%async_computation.8 | async-start | bytes 4718592 | tf_op jit(solution)/shard_map/all_gather | solution.py:142
  11.9 30.1 %copy-start.50 = (f32[4,128]{1,0:T(4,128)}, f32[4,128]{1,0:T(4,128)S(1)}, u32[]{:S(2)}) copy-start(f32[4,128]{1,0:T(4,128)S(1)} %fusion.56) | copy-start | bytes 6148
  11.9 20.5 %copy-start.46 = (f32[512]{0:T(512)}, f32[512]{0:T(512)S(1)}, u32[]{:S(2)}) copy-start(f32[512]{0:T(512)S(1)} %bitcast_rsqrt_fusion.1) | copy-start | bytes 6148
  26.2 8.7 copy-start.55
  26.2 15.8 %copy-start.41 = (f32[640]{0:T(1024)}, f32[640]{0:T(1024)S(1)}, u32[]{:S(2)}) copy-start(f32[640]{0:T(1024)S(1)} %convert_add_fusion.4) | copy-start | bytes 7684
  33.9 8.2 copy-start.3
  34.4 7.9 copy-start.8
  34.7 20.8 %copy-start.25 = (f32[128,128]{1,0:T(8,128)}, f32[128,128]{1,0:T(8,128)S(1)}, u32[]{:S(2)}) copy-start(f32[128,128]{1,0:T(8,128)S(1)} %get-tuple-element.350) | copy-start | bytes 196612
  34.7 20.8 %copy-start.27 = (f32[128,128]{1,0:T(8,128)}, f32[128,128]{1,0:T(8,128)S(1)}, u32[]{:S(2)}) copy-start(f32[128,128]{1,0:T(8,128)S(1)} %get-tuple-element.351) | copy-start | bytes 196612
  42.3 9.9 %copy-start.14 = (bf16[4,128,640]{2,1,0:T(8,128)(2,1)}, bf16[4,128,640]{2,1,0:T(8,128)(2,1)S(1)}, u32[]{:S(2)}) copy-start(bf16[4,128,640]{2,1,0:T(8,128)(2,1)S(1)} %fusion.58) | copy-start | bytes 1966084
  42.7 3.4 copy-start.21
  42.7 5.0 copy-start.54
  43.6 92.0 %all-gather.14.cloned.1.call-start = ((), (), s32[]{:S(2)}) async-start(), calls=%async_computation.10 | async-start | bytes 1638400 | tf_op jit(solution)/shard_map/all_gather | solution.py:64
  44.3 118.3 %all-gather.16.cloned.1.call-start = ((), (), s32[]{:S(2)}) async-start(), calls=%async_computation.11 | async-start | bytes 3276800 | tf_op jit(solution)/shard_map/all_gather | solution.py:65
  44.9 144.7 %all-gather.18.cloned.1.call-start = ((), (), s32[]{:S(2)}) async-start(), calls=%async_computation.12 | async-start | bytes 3276800 | tf_op jit(solution)/shard_map/all_gather | solution.py:66
  45.5 171.1 %all-gather.20.cloned.1.call-start = ((), (), s32[]{:S(2)}) async-start(), calls=%async_computation.13 | async-start | bytes 3276800 | tf_op jit(solution)/shard_map/all_gather | solution.py:67
  46.1 222.1 %all-gather.22.cloned.1.call-start = ((), (), s32[]{:S(2)}) async-start(), calls=%async_computation.14 | async-start | bytes 2359296 | tf_op jit(solution)/shard_map/all_gather | solution.py:233
  46.8 271.3 %all-gather.24.cloned.1.call-start = ((), (), s32[]{:S(2)}) async-start(), calls=%async_computation.23 | async-start | bytes 2359296 | tf_op jit(solution)/shard_map/all_gather | solution.py:232
  47.6 346.1 %reduce-scatter.17.cloned.1.call-start = ((), (), s32[]{:S(2)}) async-start(), calls=%async_computation.19 | async-start | bytes 1638400 | tf_op jit(solution)/shard_map/reduce_scatter | solution.py:292
  47.6 7.6 copy-start.57
  117.6 3.4 copy-start.22
  135.6 2.8 copy-start.4
  216.7 4.4 copy-start.16
  216.7 7.1 copy-start.65
  216.7 7.1 copy-start.68
  223.7 5.4 copy-start.33
  224.3 4.9 copy-start.60
  229.2 3.2 copy-start.61
  251.0 146.8 %reduce-scatter.11.cloned.1.call-start = ((), (), s32[]{:S(2)}) async-start(), calls=%async_computation.16 | async-start | bytes 1638400 | tf_op jit(solution)/shard_map/reduce_scatter | solution.py:283
  323.5 2.4 copy-start.63
  372.6 62.5 %reduce-scatter.19.cloned.1.call-start = ((), (), s32[]{:S(2)}) async-start(), calls=%async_computation.20 | async-start | bytes 3276800 | tf_op jit(solution)/shard_map/reduce_scatter | solution.py:295
  377.3 95.1 %reduce-scatter.21.cloned.1.call-start = ((), (), s32[]{:S(2)}) async-start(), calls=%async_computation.21 | async-start | bytes 3276800 | tf_op jit(solution)/shard_map/reduce_scatter | solution.py:298
  382.4 127.2 %reduce-scatter.23.cloned.1.call-start = ((), (), s32[]{:S(2)}) async-start(), calls=%async_computation.22 | async-start | bytes 3276800 | tf_op jit(solution)/shard_map/reduce_scatter | solution.py:301
  388.4 274.5 %reduce-scatter.9.cloned.1.call-start = ((), (), s32[]{:S(2)}) async-start(), calls=%async_computation.15 | async-start | bytes 9437184 | tf_op jit(solution)/shard_map/reduce_scatter | solution.py:260
  389.0 296.3 %reduce-scatter.15.cloned.1.call-start = ((), (), s32[]{:S(2)}) async-start(), calls=%async_computation.18 | async-start | bytes 409600 | tf_op jit(solution)/shard_map/reduce_scatter | solution.py:289
  393.7 271.8 %copy-start.9 = (f32[512,256]{1,0:T(8,128)S(1)}, f32[512,256]{1,0:T(8,128)}, u32[]{:S(2)}) copy-start(f32[512,256]{1,0:T(8,128)} %copy-done.8) | copy-start | bytes 1572868
  393.7 271.9 %copy-start.49 = (f32[4,128]{1,0:T(4,128)S(1)}, f32[4,128]{1,0:T(4,128)}, u32[]{:S(2)}) copy-start(f32[4,128]{1,0:T(4,128)} %copy-done.48) | copy-start | bytes 6148
  393.7 271.9 %copy-start.56 = (f32[256]{0:T(256)S(1)}, f32[256]{0:T(256)}, u32[]{:S(2)}) copy-start(f32[256]{0:T(256)} %copy-done.55) | copy-start | bytes 3076
  665.5 43.4 %reduce-scatter.13.cloned.1.call-start = ((), (), s32[]{:S(2)}) async-start(), calls=%async_computation.17 | async-start | bytes 409600 | tf_op jit(solution)/shard_map/reduce_scatter | solution.py:286
  666.0 2.9 copy-start.5
  666.0 2.9 copy-start.18
  666.1 2.9 copy-start.42
  666.1 2.9 copy-start.47
  669.0 10.4 %copy-start.51 = (f32[4,128]{1,0:T(4,128)S(1)}, f32[4,128]{1,0:T(4,128)}, u32[]{:S(2)}) copy-start(f32[4,128]{1,0:T(4,128)} %copy-done.50) | copy-start | bytes 6148
  669.0 10.4 %copy-start.13 = (f32[512,640]{1,0:T(8,128)S(1)}, f32[512,640]{1,0:T(8,128)}, u32[]{:S(2)}) copy-start(f32[512,640]{1,0:T(8,128)} %copy-done.12) | copy-start | bytes 3932164
  679.2 29.7 %copy-start.35 = (bf16[160,2048]{1,0:T(8,128)(2,1)S(1)}, bf16[160,2048]{1,0:T(8,128)(2,1)}, u32[]{:S(2)}) copy-start(bf16[160,2048]{1,0:T(8,128)(2,1)} %reduce-scatter.19.cloned.1.call-done) | copy-start | bytes 1966084
  679.2 29.7 %copy-start.36 = (bf16[160,2048]{1,0:T(8,128)(2,1)S(1)}, bf16[160,2048]{1,0:T(8,128)(2,1)}, u32[]{:S(2)}) copy-start(bf16[160,2048]{1,0:T(8,128)(2,1)} %reduce-scatter.21.cloned.1.call-done) | copy-start | bytes 1966084
  (40 other events, 62.8 us)
Sparse Core Ops, SparseCore 0:
  9.6 21.7 all-gather.11
  43.7 73.8 all-gather.9
  119.1 16.4 all-gather.13
  137.0 25.5 all-gather.15
  164.0 25.5 all-gather.17
  191.1 25.5 all-gather.19
  218.8 49.2 all-gather.21
  270.3 47.7 all-gather.23
  320.7 25.0 reduce-scatter.16
  372.7 25.0 reduce-scatter.10
  400.4 34.6 reduce-scatter.18
  437.7 34.6 reduce-scatter.20
  474.9 34.6 reduce-scatter.22
  513.5 149.3 reduce-scatter.8
  665.9 19.4 reduce-scatter.14
  688.4 20.4 reduce-scatter.12
